TPU v7x, 512 devices: a whole 4x4x16 slice. The times are simulated.
512 devices in a mesh: row: 16 (over y_lo, x, core), col: 32 (over y_hi, z).
Axes of the slice: x: 4, y: 4 (y_hi: 2, y_lo: 2; y = y_hi * 2 + y_lo), z: 16, core: 2. Of those that a mesh axis runs over, the one named last changes fastest.
Arguments:
- p_blocks: bfloat16 [1024, 128, 256], P(('row', 'col')), may hold values from -0.5 to 0.5
- a_blocks: bfloat16 [1024, 4096, 128], P('row', 'col'), may hold values from -6 to 6
- a_owner: int32 [16, 512], P('row', 'col'), may hold values from 0 to 31
- a_row: int32 [512, 64], P('row', 'col'), may hold values from 0 to 1
- a_count: int32 [256, 64], P('row', 'col'), may hold values from 0 to 2, as said below
Outputs:
- coarse_op: bfloat16 [256, 8192, 256], P('row', 'col')
Inputs may be any that keep to these rules, and one draw needn't show every extreme that they name: `a_count`: live blocks of one bucket are at most 2, and 2 is reached in every draw; the live load differs from tile to tile.
All inputs are finite; a program needn't handle non-finite values.
Results may differ from a plain program's by a relative error of at most 0.0049.
Values may be sent and summed in bfloat16 or wider, within the bound.
No kernel may reach another device: no remote copies, remote signals or barrier semaphores. Data moves between devices by JAX's collectives and lax.ppermute only.
A program may use at most 64 MiB of HBM per device.

v0:
```python
import jax
import jax.numpy as jnp
from jax import lax
from jax.sharding import PartitionSpec as P


def on_device(p_blocks, a_blocks, a_owner, a_row, a_count):
    groups = lax.axis_size("row")
    fine_count = p_blocks.shape[0]
    block_size = p_blocks.shape[1]
    coarse_width = p_blocks.shape[2]
    capacity = a_row.shape[1]
    panels = lax.all_gather(p_blocks, "col", axis=0, tiled=True)
    picked = a_owner.reshape(groups, 1, 1) * fine_count + a_row.reshape(
        groups, fine_count, capacity
    )
    chosen = jnp.take(panels, picked, axis=0)
    tile_blocks = a_blocks.reshape(groups, fine_count, capacity, block_size, block_size)
    slot_terms = lax.dot_general(
        tile_blocks,
        chosen,
        (((3,), (3,)), ((0, 1, 2), (0, 1, 2))),
        preferred_element_type=jnp.float32,
    )
    is_live = jnp.arange(capacity, dtype=jnp.int32)[None, None, :] < a_count[:, :, None]
    slot_terms = jnp.where(is_live[..., None, None], slot_terms, 0.0).astype(jnp.bfloat16)
    arrived = lax.all_to_all(slot_terms, "row", split_axis=0, concat_axis=0, tiled=True)
    spread = jnp.broadcast_to(
        p_blocks.reshape(fine_count, 1, block_size, coarse_width),
        (fine_count, capacity, block_size, coarse_width),
    )
    result = lax.dot_general(
        arrived, spread, (((1, 2, 3), (0, 1, 2)), ((), ())), preferred_element_type=jnp.float32
    )
    return result.astype(jnp.bfloat16)


def solution(mesh):
    in_specs = (
        P(("row", "col"), None, None),
        P("row", "col", None),
        P("row", "col"),
        P("row", "col"),
        P("row", "col"),
    )
    out_specs = P("row", "col", None)
    return jax.shard_map(
        on_device, mesh=mesh, in_specs=in_specs, out_specs=out_specs, check_vma=False
    )
```

profile of v0, /device:TPU:1, one launch (start us, length us, event | category | flops | bytes accessed | tf_op | source)
XLA Modules:
  0.0 258.3 jit_solution(17478261765161315398)
XLA Ops:
  6.5 0.0 copy-start
  6.5 0.0 all-gather.2.cloned.1.call-start
  6.5 0.7 all-gather.2.cloned.1.call-update
  7.3 0.8 reshape.50
  8.0 0.8 reshape.49
  8.8 0.8 copy.17
  9.6 0.7 multiply_bitcast_fusion
  10.2 0.1 compare_select_fusion
  10.3 0.2 copy.20
  10.5 0.1 reshape.54
  10.6 0.1 copy.18
  10.7 0.1 copy.19
  10.8 0.1 iota_compare_fusion
  10.9 161.0 %all-gather.2.cloned.1.call-done = bf16[64,128,256]{2,1,0:T(8,128)(2,1)} async-done(((bf16[2,128,256]{2,1,0:T(8,128)(2,1)}), bf16[64,128,256]{2,1,0:T(8,128)(2,1)}) %all-gather.2.cloned.1.call-update) | async-done | bytes 4194320 | tf_op jit(solution)/shard_map/all_gather | solution.py:13
  171.9 4.9 %gather_fusion = bf16[64,128,256]{2,1,0:T(8,128)(2,1)} fusion(bf16[64,128,256]{2,1,0:T(8,128)(2,1)} %all-gather.2.cloned.1.call-done, s32[1024]{0:T(1024)S(1)} %pad_clamp_fusion), kind=kCustom, calls=%fused_computation | custom fusion | bytes 8388864 | tf_op jit(solution)/shard_map/jit(_take)/gather | solution.py:17
  176.8 6.4 %copy.21 = bf16[16,2,2,128,256]{3,4,2,1,0:T(8,128)(2,1)} copy(bf16[16,2,2,128,256]{4,3,2,1,0:T(8,128)(2,1)} %bitcast.24) | data formatting | bytes 8388608 | tf_op jit(solution)/shard_map/jit(_take)/gather | solution.py:17
  183.3 0.0 copy-done
  183.3 3.5 %fusion = bf16[16,2,2,128,256]{3,4,2,1,0:T(8,128)(2,1)S(1)} fusion(pred[16,2,2]{2,1,0:T(4,128)(4,1)S(1)} %iota_compare_fusion, bf16[16,2,2,128,128]{4,3,2,1,0:T(8,128)(2,1)S(1)} %bitcast.23, bf16[16,2,2,128,256]{3,4,2,1,0:T(8,128)(2,1)} %copy.21, pred[16,2,2]{2,1,0:T(4,128)(4,1)S(1)} %copy.19), kind=kOutput, calls=%fused_computation.2 | convolution fusion | flops 543162368 | bytes 10485888 | tf_op jit(solution)/shard_map/dot_general | solution.py:19
  186.8 0.0 copy-start.1
  186.8 62.1 %all_to_all.5 = bf16[16,2,2,128,256]{3,4,2,1,0:T(8,128)(2,1)S(1)} all-to-all(bf16[16,2,2,128,256]{3,4,2,1,0:T(8,128)(2,1)S(1)} %fusion), channel_id=1, replica_groups=mesh['row'=16,'col'=32] {'row'}, dimensions={0} | all-to-all | bytes 8388608 | tf_op jit(solution)/shard_map/all_to_all | solution.py:27
  248.9 0.0 copy-done.1
  248.9 2.6 bitcast_convert_fusion
  (2 shorter events, 0.0 us)
Async XLA Ops:
  6.5 176.7 %copy-start = (bf16[64,128,128]{2,1,0:T(8,128)(2,1)S(1)}, bf16[64,128,128]{2,1,0:T(8,128)(2,1)}, u32[]{:S(2)}) copy-start(bf16[64,128,128]{2,1,0:T(8,128)(2,1)} %param.6) | copy-start | bytes 6291460
  6.5 165.4 %all-gather.2.cloned.1.call-start = ((), (), s32[]{:S(2)}) async-start(), calls=%async_computation.1 | async-start | bytes 4325376 | tf_op jit(solution)/shard_map/all_gather | solution.py:13
  186.8 62.1 %copy-start.1 = (bf16[2,128,256]{2,1,0:T(8,128)(2,1)S(1)}, bf16[2,128,256]{2,1,0:T(8,128)(2,1)}, u32[]{:S(2)}) copy-start(bf16[2,128,256]{2,1,0:T(8,128)(2,1)} %param.5) | copy-start | bytes 393220
Sparse Core Ops, SparseCore 0:
  10.5 161.3 all-gather.1
where the time goes:
time: 259 us; the launch traced here: 258 us
  waiting for transfers between devices  162 us (63%)
  blocking collectives  62.1 us (24%)
  local copies, waits for them, and re-layouts  14.2 us (5%)
  between operations  13.4 us (5%)
  matrix products  6.07 us (2%)
    all_gather x1, waiting for transfers between devices, on_device(): panels = lax.all_gather(p_blocks, 'col', axis=0, tiled=True)  161 us
    all_to_all x1, blocking collectives, on_device(): lax.all_to_all(slot_terms, 'row', split_axis=0, concat_axis=0, tiled=True)  62.1 us
    gather x2, local copies, waits for them, and re-layouts, on_device(): chosen = jnp.take(panels, picked, axis=0)  11.4 us
  transfers between devices with their start and end apart: 1, of which 1 were waited for; matrix products, arithmetic and copies ran while one was open for 1% of the time, Pallas kernels for 0%

commit v1 on v0

--- a/solution.py
+++ b/solution.py
@@ -2,6 +2,10 @@
 import jax.numpy as jnp
 from jax import lax
 from jax.sharding import PartitionSpec as P
+
+bring_case_over_axis = lambda my_tile, which_axis: jnp.concatenate(
+    lax.all_to_all(jnp.stack(lax.psum(1, which_axis) * [my_tile], axis=0), which_axis, 0, 0), axis=0
+)
 
 
 def on_device(p_blocks, a_blocks, a_owner, a_row, a_count):
@@ -10,7 +14,7 @@
     block_size = p_blocks.shape[1]
     coarse_width = p_blocks.shape[2]
     capacity = a_row.shape[1]
-    panels = lax.all_gather(p_blocks, "col", axis=0, tiled=True)
+    panels = bring_case_over_axis(p_blocks, "col")
     picked = a_owner.reshape(groups, 1, 1) * fine_count + a_row.reshape(
         groups, fine_count, capacity
     )

time: 259 us -> 285 us (1.10); the launches traced: 258 us -> 281 us
  waiting for transfers between devices: 162 us -> 185 us
  starting transfers between devices: 0.01 us -> 18.9 us
  between operations: 13.4 us -> 0.08 us
  blocking collectives: 62.1 us -> 55.2 us
    all_to_all x0 -> x1, waiting for transfers between devices: none -> 185 us  [lax.all_to_all(jnp.stack(lax.psum(1, which_axis) * [my_tile], axis=0), wh...]
    all_gather x1 -> x0, waiting for transfers between devices: 161 us -> none  [on_device(): panels = lax.all_gather(p_blocks, 'col', axis=0, tiled=True)]
    all_to_all x0 -> x1, starting transfers between devices: none -> 18.9 us  [lax.all_to_all(jnp.stack(lax.psum(1, which_axis) * [my_tile], axis=0), wh...]
    all_to_all x1, blocking collectives: 62.1 us -> 55.2 us  [on_device(): lax.all_to_all(slot_terms, 'row', split_axis=0, concat_axis=0, tiled=True)]
    another operation x0 -> x1, local copies, waits for them, and re-layouts: none -> 3.53 us  [jnp.stack(lax.psum(1, which_axis) * [my_tile], axis=0)]
  transfers between devices with their start and end apart: 1 -> 1, of which waited for: 1 -> 1; matrix products, arithmetic and copies ran while one was open for 1% -> 0% of each run, Pallas kernels for 0% -> 0%
where the time goes in v1:
time: 285 us; the launch traced here: 281 us
  waiting for transfers between devices  185 us (65%)
  blocking collectives  55.2 us (19%)
  starting transfers between devices  18.9 us (7%)
  local copies, waits for them, and re-layouts  15.7 us (6%)
  matrix products  6.07 us (2%)
    all_to_all x1, waiting for transfers between devices, lax.all_to_all(jnp.stack(lax.psum(1, which_axis) * [my_tile], axis=0), wh...  185 us
    all_to_all x1, blocking collectives, on_device(): lax.all_to_all(slot_terms, 'row', split_axis=0, concat_axis=0, tiled=True)  55.2 us
    all_to_all x1, starting transfers between devices, lax.all_to_all(jnp.stack(lax.psum(1, which_axis) * [my_tile], axis=0), wh...  18.9 us
    gather x2, local copies, waits for them, and re-layouts, on_device(): chosen = jnp.take(panels, picked, axis=0)  11.4 us
  transfers between devices with their start and end apart: 1, of which 1 were waited for; matrix products, arithmetic and copies ran while one was open for 0% of the time, Pallas kernels for 0%

profile of v1, /device:TPU:1, one launch (start us, length us, event | category | flops | bytes accessed | tf_op | source)
XLA Modules:
  0.0 280.6 jit_solution(15193298624204147795)
XLA Ops:
  0.0 0.0 copy-start
  0.0 3.5 %stack.2 = bf16[32,2,128,256]{3,2,1,0:T(8,128)(2,1)} broadcast(bf16[2,128,256]{2,1,0:T(8,128)(2,1)} %param.5), dimensions={1,2,3} | broadcast | bytes 4325376 | tf_op jit(solution)/shard_map/stack | solution.py:7
  3.5 18.9 %all-to-all-start = ((bf16[32,2,128,256]{3,2,1,0:T(8,128)(2,1)}), bf16[32,2,128,256]{3,2,1,0:T(8,128)(2,1)}, u32[]{:S(2)}, u32[]{:S(2)}) async-start(bf16[32,2,128,256]{3,2,1,0:T(8,128)(2,1)} %stack.2), calls=%async_computation | async-start | bytes 8388608 | tf_op jit(solution)/shard_map/all_to_all | solution.py:7
  22.5 0.0 copy-done.2
  22.5 0.1 reshape.56
  22.6 0.1 reshape.54
  22.6 0.0 copy-done.4
  22.7 0.1 compare_select_fusion
  22.7 0.2 copy.20
  23.0 0.1 reshape.60
  23.1 0.1 copy.18
  23.2 0.1 copy.19
  23.3 0.0 copy-done.3
  23.3 0.1 copy.17
  23.4 0.1 iota_compare_fusion
  23.5 184.5 %all-to-all-done = bf16[32,2,128,256]{3,2,1,0:T(8,128)(2,1)} async-done(((bf16[32,2,128,256]{3,2,1,0:T(8,128)(2,1)}), bf16[32,2,128,256]{3,2,1,0:T(8,128)(2,1)}, u32[]{:S(2)}, u32[]{:S(2)}) %all-to-all-start) | async-done | bytes 4194336 | tf_op jit(solution)/shard_map/all_to_all | solution.py:7
  208.0 5.0 %gather_fusion = bf16[64,128,256]{2,1,0:T(8,128)(2,1)} fusion(bf16[64,128,256]{2,1,0:T(8,128)(2,1)} %bitcast.1, s32[1024]{0:T(1024)S(1)} %pad_clamp_fusion), kind=kCustom, calls=%fused_computation | custom fusion | bytes 8388864 | tf_op jit(solution)/shard_map/jit(_take)/gather | solution.py:21
  213.0 6.4 %copy.21 = bf16[16,2,2,128,256]{3,4,2,1,0:T(8,128)(2,1)} copy(bf16[16,2,2,128,256]{4,3,2,1,0:T(8,128)(2,1)} %bitcast.25) | data formatting | bytes 8388608 | tf_op jit(solution)/shard_map/jit(_take)/gather | solution.py:21
  219.3 0.0 copy-done
  219.3 3.5 %fusion = bf16[16,2,2,128,256]{3,4,2,1,0:T(8,128)(2,1)S(1)} fusion(pred[16,2,2]{2,1,0:T(4,128)(4,1)S(1)} %iota_compare_fusion, bf16[16,2,2,128,128]{4,3,2,1,0:T(8,128)(2,1)S(1)} %bitcast.24, bf16[16,2,2,128,256]{3,4,2,1,0:T(8,128)(2,1)} %copy.21, pred[16,2,2]{2,1,0:T(4,128)(4,1)S(1)} %copy.19), kind=kOutput, calls=%fused_computation.2 | convolution fusion | flops 543162368 | bytes 10485888 | tf_op jit(solution)/shard_map/dot_general | solution.py:23
  222.9 0.0 copy-start.1
  222.9 55.2 %all_to_all.10 = bf16[16,2,2,128,256]{3,4,2,1,0:T(8,128)(2,1)S(1)} all-to-all(bf16[16,2,2,128,256]{3,4,2,1,0:T(8,128)(2,1)S(1)} %fusion), channel_id=1, replica_groups=mesh['row'=16,'col'=32] {'row'}, dimensions={0} | all-to-all | bytes 8388608 | tf_op jit(solution)/shard_map/all_to_all | solution.py:31
  278.0 0.0 copy-done.1
  278.0 2.6 bitcast_convert_fusion
  (6 shorter events, 0.0 us)
Async XLA Ops:
  0.0 219.3 %copy-start = (bf16[64,128,128]{2,1,0:T(8,128)(2,1)S(1)}, bf16[64,128,128]{2,1,0:T(8,128)(2,1)}, u32[]{:S(2)}) copy-start(bf16[64,128,128]{2,1,0:T(8,128)(2,1)} %param.6) | copy-start | bytes 6291460
  3.5 18.9 %copy-start.2 = (s32[32,2]{0,1:T(2,128)S(1)}, s32[32,2]{0,1:T(2,128)}, u32[]{:S(2)}) copy-start(s32[32,2]{0,1:T(2,128)} %param.8) | copy-start | bytes 772
  3.5 19.1 %copy-start.4 = (s32[1,16]{1,0:T(1,128)S(1)}, s32[1,16]{1,0:T(1,128)}, u32[]{:S(2)}) copy-start(s32[1,16]{1,0:T(1,128)} %param.7) | copy-start | bytes 196
  3.5 19.8 %copy-start.3 = (s32[16,2]{0,1:T(2,128)S(1)}, s32[16,2]{0,1:T(2,128)}, u32[]{:S(2)}) copy-start(s32[16,2]{0,1:T(2,128)} %param.9) | copy-start | bytes 388
  3.5 204.4 %all-to-all-start = ((bf16[32,2,128,256]{3,2,1,0:T(8,128)(2,1)}), bf16[32,2,128,256]{3,2,1,0:T(8,128)(2,1)}, u32[]{:S(2)}, u32[]{:S(2)}) async-start(bf16[32,2,128,256]{3,2,1,0:T(8,128)(2,1)} %stack.2), calls=%async_computation | async-start | bytes 8388608 | tf_op jit(solution)/shard_map/all_to_all | solution.py:7
  222.9 55.2 %copy-start.1 = (bf16[2,128,256]{2,1,0:T(8,128)(2,1)S(1)}, bf16[2,128,256]{2,1,0:T(8,128)(2,1)}, u32[]{:S(2)}) copy-start(bf16[2,128,256]{2,1,0:T(8,128)(2,1)} %param.5) | copy-start | bytes 393220
